TPU v7x, 32 devices: a whole 2x2x4 slice. The times are simulated.
32 devices in a mesh: crops: 8 (over z, x), rows: 4 (over y, core).
Axes of the slice: x: 2, y: 2, z: 4, core: 2. Of those that a mesh axis runs over, the one named last changes fastest.
Arguments:
- features: bfloat16 [640, 8, 8, 2048], P('crops', 'rows'), may hold values from -6 to 6
- pixel_mask: int32 [640, 8, 8], P('crops', 'rows'), may hold values from 0 to 1, as said below
- partners: int32 [640], P('crops'), may hold values from 0 to 639, as said below
- queued: float32 [3840, 128], P(('crops', 'rows')), as said below
- w_reduce: bfloat16 [2048, 512], P('crops'), may hold values from -0.125 to 0.125
- w_spatial: bfloat16 [4608, 512], P('crops'), may hold values from -0.09375 to 0.09375
- w_expand: bfloat16 [512, 2048], P('crops'), may hold values from -0.25 to 0.25
- w_hidden: bfloat16 [2048, 2048], P('crops'), may hold values from -0.125 to 0.125
- w_embed: bfloat16 [2048, 128], P('crops'), may hold values from -0.125 to 0.125
- prototypes: float32 [128, 3000], replicated, may hold values from -0.75 to 0.75
- gain_one: float32 [512], replicated, may hold values from 0.1 to 1.9
- bias_one: float32 [512], replicated, may hold values from -2.5 to 2.5
- gain_two: float32 [512], replicated, may hold values from 0.1 to 1.9
- bias_two: float32 [512], replicated, may hold values from -2.5 to 2.5
- gain_three: float32 [2048], replicated, may hold values from 0.1 to 1.9
- bias_three: float32 [2048], replicated, may hold values from -2.5 to 2.5
- gain_head: float32 [2048], replicated, may hold values from 0.1 to 1.9
- bias_head: float32 [2048], replicated, may hold values from -2.5 to 2.5
Outputs:
- swav_loss: float32 [], replicated
- grad_features: bfloat16 [640, 8, 8, 2048], P('crops', 'rows')
- grad_w_reduce: float32 [2048, 512], P('crops')
- grad_w_spatial: float32 [4608, 512], P('crops')
- grad_w_expand: float32 [512, 2048], P('crops')
- grad_w_hidden: float32 [2048, 2048], P('crops')
- grad_w_embed: float32 [2048, 128], P('crops')
- grad_prototypes: float32 [128, 3000], replicated
- grad_gain_one: float32 [512], replicated
- grad_bias_one: float32 [512], replicated
- grad_gain_two: float32 [512], replicated
- grad_bias_two: float32 [512], replicated
- grad_gain_three: float32 [2048], replicated
- grad_bias_three: float32 [2048], replicated
- grad_gain_head: float32 [2048], replicated
- grad_bias_head: float32 [2048], replicated
Inputs may be any that keep to these rules, and one draw needn't show every extreme that they name: `pixel_mask`: each crop's valid pixels form one rectangle of 7 x 7 or 6 x 8 pixels inside its map. partners[n] != n, partners[partners[n]] == n, and n and partners[n] lie in the same aligned block of 80 crops. `queued`: every row has a nonzero entry.
All inputs are finite; a program needn't handle non-finite values.
Results may differ from a plain program's by a relative error of at most 0.012.
Values may be sent and summed in bfloat16 or wider, within the bound.
No kernel may reach another device: no remote copies, remote signals or barrier semaphores. Data moves between devices by JAX's collectives and lax.ppermute only.
A program may use at most 192 MiB of HBM per device.

v0:
```python
import jax
import jax.numpy as jnp
from jax import lax
from jax.sharding import PartitionSpec as P

EPS_NORM = 1e-05
EPS_UNIT = 1e-06
SHARPNESS = 0.05
SOFTMAX_TEMPER = 0.1
PRECISE = lax.Precision.HIGHEST


def with_halo(cells, sides, width):
    for axis, dim in sides:
        count = lax.axis_size(axis)
        ends = count - 1
        head = lax.slice_in_dim(cells, 0, width, axis=dim)
        tail = lax.slice_in_dim(cells, cells.shape[dim] - width, cells.shape[dim], axis=dim)
        cells = jnp.concatenate(
            [
                lax.ppermute(tail, axis, [(i, (i + 1) % count) for i in range(ends)]),
                cells,
                lax.ppermute(head, axis, [((i + 1) % count, i) for i in range(ends)]),
            ],
            axis=dim,
        )
    return cells


def moments(value_entries, weights):
    first_sum = jnp.sum(value_entries * weights, axis=0)
    second_sum = jnp.sum(value_entries * value_entries * weights, axis=0)
    total_sum, square_sum, valid_count = lax.psum(
        (first_sum, second_sum, jnp.sum(weights)), ("crops", "rows")
    )
    col_mean = total_sum / valid_count
    spread = lax.rsqrt(square_sum / valid_count - col_mean * col_mean + EPS_NORM)
    return (col_mean, spread, valid_count)


def norm_back(upstream, normed, weights, gain, spread, valid_count):
    grad_gain, grad_bias = lax.psum(
        (jnp.sum(upstream * normed, axis=0), jnp.sum(upstream, axis=0)), ("crops", "rows")
    )
    grad_input = (
        weights * (gain * spread) * (upstream - (grad_bias + normed * grad_gain) / valid_count)
    )
    return (grad_input, grad_gain, grad_bias)


def gelu_back(inputs, upstream):
    return jax.vjp(jax.nn.gelu, inputs)[1](upstream)[0]


def tap_columns(extended, height, breadth):
    padded = jnp.pad(extended, ((0, 0), (0, 0), (1, 1), (0, 0)))
    pieces = [
        padded[:, tap_row : tap_row + height, tap_col : tap_col + breadth, :]
        for tap_row in range(3)
        for tap_col in range(3)
    ]
    return jnp.concatenate(pieces, axis=-1).reshape(-1, 9 * extended.shape[3])


def block_forward(features, pixel_mask, weights, params, kept_stats):
    w_reduce, w_spatial, w_expand = weights
    gain_one, bias_one, gain_two, bias_two, gain_three, bias_three = params
    local_crops, height, breadth, channels = features.shape
    masked = features * pixel_mask.astype(jnp.bfloat16)[..., None]
    flat_in = masked.reshape(-1, channels)
    weight_col = pixel_mask.reshape(-1, 1).astype(jnp.float32)
    pre_one = jnp.dot(flat_in, w_reduce, preferred_element_type=jnp.float32)
    stat_one = moments(pre_one, weight_col) if kept_stats is None else kept_stats[0]
    norm_one = (pre_one - stat_one[0]) * stat_one[1]
    act_one = gain_one * norm_one + bias_one
    hidden_one = (jax.nn.gelu(act_one) * weight_col).astype(jnp.bfloat16)
    grid_one = hidden_one.reshape(local_crops, height, breadth, -1)
    extended = with_halo(grid_one, (("rows", 1),), 1)
    columns = tap_columns(extended, height, breadth)
    pre_two = jnp.dot(columns, w_spatial, preferred_element_type=jnp.float32)
    stat_two = moments(pre_two, weight_col) if kept_stats is None else kept_stats[1]
    norm_two = (pre_two - stat_two[0]) * stat_two[1]
    act_two = gain_two * norm_two + bias_two
    hidden_two = (jax.nn.gelu(act_two) * weight_col).astype(jnp.bfloat16)
    pre_three = jnp.dot(hidden_two, w_expand, preferred_element_type=jnp.float32)
    stat_three = moments(pre_three, weight_col) if kept_stats is None else kept_stats[2]
    norm_three = (pre_three - stat_three[0]) * stat_three[1]
    summed = gain_three * norm_three + bias_three + flat_in.astype(jnp.float32)
    output = jax.nn.gelu(summed) * weight_col
    kept = (
        flat_in,
        weight_col,
        columns,
        norm_one,
        act_one,
        norm_two,
        act_two,
        hidden_two,
        norm_three,
        summed,
        output,
    )
    return (kept, (stat_one, stat_two, stat_three))


def shards(
    features,
    pixel_mask,
    partners,
    queued,
    w_reduce,
    w_spatial,
    w_expand,
    w_hidden,
    w_embed,
    prototypes,
    gain_one,
    bias_one,
    gain_two,
    bias_two,
    gain_three,
    bias_three,
    gain_head,
    bias_head,
):
    full_reduce, full_spatial, full_expand, full_hidden, full_embed = (
        lax.all_gather(w_reduce, "crops", axis=0, tiled=True),
        lax.all_gather(w_spatial, "crops", axis=0, tiled=True),
        lax.all_gather(w_expand, "crops", axis=0, tiled=True),
        lax.all_gather(w_hidden, "crops", axis=0, tiled=True),
        lax.all_gather(w_embed, "crops", axis=0, tiled=True),
    )
    block_weights = (full_reduce, full_spatial, full_expand)
    block_params = (gain_one, bias_one, gain_two, bias_two, gain_three, bias_three)
    local_crops, height, breadth, channels = features.shape
    kept, stats = block_forward(features, pixel_mask, block_weights, block_params, None)
    output = kept[10]
    crop_sums = jnp.sum(output.reshape(local_crops, height * breadth, channels), axis=1)
    crop_valid = jnp.sum(pixel_mask.reshape(local_crops, -1), axis=1).astype(jnp.float32)
    pooled_sum, crop_count = (
        lax.psum_scatter(crop_sums, "rows", scatter_dimension=0, tiled=True),
        lax.psum_scatter(crop_valid, "rows", scatter_dimension=0, tiled=True),
    )
    pooled = pooled_sum / crop_count[:, None]
    head_matrix = full_hidden.astype(jnp.float32)
    embed_matrix = full_embed.astype(jnp.float32)
    pre_head = jnp.dot(pooled, head_matrix, precision=PRECISE)
    head_ones = jnp.ones((pre_head.shape[0], 1), jnp.float32)
    stat_head = moments(pre_head, head_ones)
    norm_head = (pre_head - stat_head[0]) * stat_head[1]
    projector_activation = gain_head * norm_head + bias_head
    hidden_head = jax.nn.gelu(projector_activation)
    embedding = jnp.dot(hidden_head, embed_matrix, precision=PRECISE)
    inverse = lax.rsqrt(jnp.sum(embedding * embedding, axis=1, keepdims=True) + EPS_UNIT)
    unit_embed = embedding * inverse
    centroid_similarity = jnp.dot(unit_embed, prototypes, precision=PRECISE)
    queue_unit = queued * lax.rsqrt(jnp.sum(queued * queued, axis=1, keepdims=True) + EPS_UNIT)
    stored_similarity = jnp.dot(queue_unit, prototypes, precision=PRECISE)
    total_crops = local_crops * lax.axis_size("crops")
    row_total = total_crops + queued.shape[0] * lax.axis_size("crops") * lax.axis_size("rows")
    proto_total = centroid_similarity.shape[1]
    plan_mass = jnp.exp(centroid_similarity / SHARPNESS)
    queue_mass = jnp.exp(stored_similarity / SHARPNESS)
    for iteration in range(3):
        column = lax.psum(
            jnp.sum(plan_mass, axis=0) + jnp.sum(queue_mass, axis=0), ("crops", "rows")
        )
        plan_mass = plan_mass / (proto_total * column)
        queue_mass = queue_mass / (proto_total * column)
        plan_mass = plan_mass / (row_total * jnp.sum(plan_mass, axis=1, keepdims=True))
        queue_mass = queue_mass / (row_total * jnp.sum(queue_mass, axis=1, keepdims=True))
    balanced_cluster_labels = row_total * plan_mass
    everyone = lax.all_gather(balanced_cluster_labels, "rows", axis=0, tiled=True)
    share_rows = balanced_cluster_labels.shape[0]
    partner_rows = (
        lax.dynamic_slice_in_dim(partners, lax.axis_index("rows") * share_rows, share_rows)
        - lax.axis_index("crops") * local_crops
    )
    swapped_cluster_labels = jnp.take(everyone, partner_rows, axis=0)
    log_probability = jax.nn.log_softmax(centroid_similarity / SOFTMAX_TEMPER, axis=1)
    loss_part = -jnp.sum(swapped_cluster_labels * log_probability) / total_crops
    grad_scores = (
        jnp.exp(log_probability) * jnp.sum(swapped_cluster_labels, axis=1, keepdims=True)
        - swapped_cluster_labels
    ) / (SOFTMAX_TEMPER * total_crops)
    grad_proto_part = jnp.dot(unit_embed.T, grad_scores, precision=PRECISE)
    grad_unit = jnp.dot(grad_scores, prototypes.T, precision=PRECISE)
    grad_embedding = inverse * (
        grad_unit - unit_embed * jnp.sum(unit_embed * grad_unit, axis=1, keepdims=True)
    )
    grad_w_embed = jnp.dot(hidden_head.T, grad_embedding, precision=PRECISE)
    grad_hidden_head = jnp.dot(grad_embedding, embed_matrix.T, precision=PRECISE)
    grad_act_head = gelu_back(projector_activation, grad_hidden_head)
    grad_gain_head, grad_bias_head, grad_prototypes, swav_loss = lax.psum(
        (
            jnp.sum(grad_act_head * norm_head, axis=0),
            jnp.sum(grad_act_head, axis=0),
            grad_proto_part,
            loss_part,
        ),
        ("crops", "rows"),
    )
    grad_pre_head = (
        gain_head
        * stat_head[1]
        * (grad_act_head - (grad_bias_head + norm_head * grad_gain_head) / stat_head[2])
    )
    grad_w_hidden = jnp.dot(pooled.T, grad_pre_head, precision=PRECISE)
    grad_pooled = jnp.dot(grad_pre_head, head_matrix.T, precision=PRECISE)
    per_pixel = grad_pooled / crop_count[:, None]
    scale_rows = lax.all_gather(per_pixel, "rows", axis=0, tiled=True)
    kept, stats = block_forward(features, pixel_mask, block_weights, block_params, stats)
    (
        flat_in,
        weight_col,
        columns,
        norm_one,
        act_one,
        norm_two,
        act_two,
        hidden_two,
        norm_three,
        summed,
        output,
    ) = kept
    stat_one, stat_two, stat_three = stats
    grad_output = (
        scale_rows[:, None, :] * weight_col.reshape(local_crops, height * breadth, 1)
    ).reshape(-1, channels)
    grad_summed = gelu_back(summed, grad_output)
    grad_pre_three, grad_gain_three, grad_bias_three = norm_back(
        grad_summed, norm_three, weight_col, gain_three, stat_three[1], stat_three[2]
    )
    grad_pre_three = grad_pre_three.astype(jnp.bfloat16)
    grad_w_expand = jnp.dot(hidden_two.T, grad_pre_three, preferred_element_type=jnp.float32)
    grad_hidden_two = jnp.dot(grad_pre_three, full_expand.T, preferred_element_type=jnp.float32)
    grad_act_two = gelu_back(act_two, grad_hidden_two * weight_col)
    grad_pre_two, grad_gain_two, grad_bias_two = norm_back(
        grad_act_two, norm_two, weight_col, gain_two, stat_two[1], stat_two[2]
    )
    grad_pre_two = grad_pre_two.astype(jnp.bfloat16)
    grad_w_spatial = jnp.dot(columns.T, grad_pre_two, preferred_element_type=jnp.float32)
    narrow = grad_pre_two.shape[1]
    grad_grid = grad_pre_two.reshape(local_crops, height, breadth, narrow)
    grad_extended = with_halo(grad_grid, (("rows", 1),), 1)
    spatial_back = (
        full_spatial.reshape(9, -1, narrow)[::-1].transpose(0, 2, 1).reshape(9 * narrow, -1)
    )
    grad_hidden_one = jnp.dot(
        tap_columns(grad_extended, height, breadth),
        spatial_back,
        preferred_element_type=jnp.float32,
    )
    grad_act_one = gelu_back(act_one, grad_hidden_one * weight_col)
    grad_pre_one, grad_gain_one, grad_bias_one = norm_back(
        grad_act_one, norm_one, weight_col, gain_one, stat_one[1], stat_one[2]
    )
    grad_pre_one = grad_pre_one.astype(jnp.bfloat16)
    grad_w_reduce = jnp.dot(flat_in.T, grad_pre_one, preferred_element_type=jnp.float32)
    grad_features = (
        (
            (jnp.dot(grad_pre_one, full_reduce.T, preferred_element_type=jnp.float32) + grad_summed)
            * weight_col
        )
        .astype(jnp.bfloat16)
        .reshape(features.shape)
    )
    sum_reduce, sum_spatial, sum_expand, sum_hidden, sum_embed = (
        lax.psum_scatter(grad_w_reduce, "crops", scatter_dimension=0, tiled=True),
        lax.psum_scatter(grad_w_spatial, "crops", scatter_dimension=0, tiled=True),
        lax.psum_scatter(grad_w_expand, "crops", scatter_dimension=0, tiled=True),
        lax.psum_scatter(grad_w_hidden, "crops", scatter_dimension=0, tiled=True),
        lax.psum_scatter(grad_w_embed, "crops", scatter_dimension=0, tiled=True),
    )
    out_reduce, out_spatial, out_expand, out_hidden, out_embed = lax.psum(
        (sum_reduce, sum_spatial, sum_expand, sum_hidden, sum_embed), "rows"
    )
    return (
        swav_loss,
        grad_features,
        out_reduce,
        out_spatial,
        out_expand,
        out_hidden,
        out_embed,
        grad_prototypes,
        grad_gain_one,
        grad_bias_one,
        grad_gain_two,
        grad_bias_two,
        grad_gain_three,
        grad_bias_three,
        grad_gain_head,
        grad_bias_head,
    )


def solution(mesh):
    in_specs = (
        P("crops", "rows", None, None),
        P("crops", "rows", None),
        P("crops"),
        P(("crops", "rows"), None),
        P("crops", None),
        P("crops", None),
        P("crops", None),
        P("crops", None),
        P("crops", None),
        P(),
        P(),
        P(),
        P(),
        P(),
        P(),
        P(),
        P(),
        P(),
    )
    out_specs = (
        P(),
        P("crops", "rows", None, None),
        P("crops", None),
        P("crops", None),
        P("crops", None),
        P("crops", None),
        P("crops", None),
        P(),
        P(),
        P(),
        P(),
        P(),
        P(),
        P(),
        P(),
        P(),
    )
    return jax.shard_map(shards, mesh=mesh, in_specs=in_specs, out_specs=out_specs, check_vma=False)
```

profile of v0, /device:TPU:0, one launch (start us, length us, event | category | flops | bytes accessed | tf_op | source)
XLA Modules:
  0.0 1608.6 jit_solution(18232524275703027354)
XLA Ops:
  18.8 43.4 %all-gather.7.cloned.1.call-done = bf16[2048,512]{1,0:T(8,128)(2,1)} async-done(((bf16[256,512]{1,0:T(8,128)(2,1)}), bf16[2048,512]{1,0:T(8,128)(2,1)}) %all-gather.7.cloned.1.call-update) | async-done | bytes 2097168 | tf_op jit(solution)/shard_map/all_gather | solution.py:127
  69.9 40.6 %all-reduce.12 = (f32[512]{0:T(512)S(1)}, f32[]{:T(128)}, f32[512]{0:T(512)S(1)}) all-reduce(f32[512]{0:T(512)S(1)} %get-tuple-element.23, f32[]{:T(128)} %convert_reduce_fusion, f32[512]{0:T(512)S(1)} %get-tuple-element.22), channel_id=1, replica_groups=mesh['crops'=8,'rows'=4] {'crops','rows'}, use_global_device_ids=true, to_apply=%region_5.0 | all-reduce | flops 1025 | bytes 8200 | tf_op jit(solution)/shard_map/psum | solution.py:33
  123.0 9.4 all-reduce.3
  133.2 34.4 %all_gather.25 = bf16[2048,128]{1,0:T(8,128)(2,1)} all-gather(bf16[256,128]{1,0:T(8,128)(2,1)S(1)} %copy-done.27), channel_id=1, replica_groups=mesh['crops'=8,'rows'=4] {'crops'}, dimensions={0}, use_global_device_ids=true | all-gather | bytes 589824 | tf_op jit(solution)/shard_map/all_gather | solution.py:131
  189.2 11.7 multiply_reduce_fusion.6
  200.8 42.9 %all-reduce.11 = (f32[512]{0:T(512)S(1)}, f32[512]{0:T(512)S(1)}) all-reduce(f32[512]{0:T(512)S(1)} %get-tuple-element.21, f32[512]{0:T(512)S(1)} %get-tuple-element.20), channel_id=1, replica_groups=mesh['crops'=8,'rows'=4] {'crops','rows'}, use_global_device_ids=true, to_apply=%region_9.10 | all-reduce | flops 1024 | bytes 8192 | tf_op jit(solution)/shard_map/psum | solution.py:33
  245.0 8.8 multiply_reduce_fusion.1
  253.8 45.8 %all-reduce.10 = (f32[2048]{0:T(1024)S(1)}, f32[2048]{0:T(1024)S(1)}) all-reduce(f32[2048]{0:T(1024)S(1)} %get-tuple-element.17, f32[2048]{0:T(1024)S(1)} %get-tuple-element.16), channel_id=1, replica_groups=mesh['crops'=8,'rows'=4] {'crops','rows'}, use_global_device_ids=true, to_apply=%region_11.12 | all-reduce | flops 4096 | bytes 32768 | tf_op jit(solution)/shard_map/psum | solution.py:33
  301.5 13.3 multiply_multiply_fusion.2
  322.0 13.7 fusion
  346.2 45.6 %all-reduce.9 = (f32[2048]{0:T(1024)S(1)}, f32[]{:T(128)}, f32[2048]{0:T(1024)S(1)}) all-reduce(f32[2048]{0:T(1024)S(1)} %get-tuple-element.37, f32[]{:T(128)} %constant.39.clone.1, f32[2048]{0:T(1024)S(1)} %get-tuple-element.36), channel_id=1, replica_groups=mesh['crops'=8,'rows'=4] {'crops','rows'}, use_global_device_ids=true, to_apply=%region_22.23 | all-reduce | flops 4097 | bytes 32776 | tf_op jit(solution)/shard_map/psum | solution.py:33
  397.5 40.5 %psum.212 = f32[3000]{0:T(1024)} all-reduce(f32[3000]{0:T(1024)} %add.273), channel_id=1, replica_groups=mesh['crops'=8,'rows'=4] {'crops','rows'}, use_global_device_ids=true, to_apply=%region_27.28 | all-reduce | flops 3000 | bytes 24000 | tf_op jit(solution)/shard_map/psum | solution.py:165
  441.3 40.8 %psum.213 = f32[3000]{0:T(1024)} all-reduce(f32[3000]{0:T(1024)} %add.274), channel_id=1, replica_groups=mesh['crops'=8,'rows'=4] {'crops','rows'}, use_global_device_ids=true, to_apply=%region_32.33 | all-reduce | flops 3000 | bytes 24000 | tf_op jit(solution)/shard_map/psum | solution.py:165
  487.2 40.9 %psum.214 = f32[3000]{0:T(1024)S(1)} all-reduce(f32[3000]{0:T(1024)S(1)} %add.275), channel_id=1, replica_groups=mesh['crops'=8,'rows'=4] {'crops','rows'}, use_global_device_ids=true, to_apply=%region_37.38 | all-reduce | flops 3000 | bytes 24000 | tf_op jit(solution)/shard_map/psum | solution.py:165
  529.9 12.0 all-gather
  549.8 37.9 %all-reduce.8 = (f32[2048]{0:T(1024)S(1)}, f32[2048]{0:T(1024)S(1)}) all-reduce(f32[2048]{0:T(1024)S(1)} %get-tuple-element.35, f32[2048]{0:T(1024)S(1)} %get-tuple-element.34), channel_id=1, replica_groups=mesh['crops'=8,'rows'=4] {'crops','rows'}, use_global_device_ids=true, to_apply=%region_48.49 | all-reduce | flops 4096 | bytes 32768 | tf_op jit(solution)/shard_map/psum | solution.py:194
  587.7 9.6 fusion.27
  597.3 9.4 all-gather.1
  607.4 15.0 fusion.82
  622.4 40.0 %all-reduce.7 = (f32[2048]{0:T(1024)S(1)}, f32[2048]{0:T(1024)S(1)}) all-reduce(f32[2048]{0:T(1024)S(1)} %get-tuple-element.19, f32[2048]{0:T(1024)S(1)} %get-tuple-element.18), channel_id=1, replica_groups=mesh['crops'=8,'rows'=4] {'crops','rows'}, use_global_device_ids=true, to_apply=%region_52.53 | all-reduce | flops 4096 | bytes 32768 | tf_op jit(solution)/shard_map/psum | solution.py:42
  662.4 10.0 multiply_convert_fusion.1
  678.7 39.6 %all-reduce.6 = (f32[512]{0:T(512)S(1)}, f32[512]{0:T(512)S(1)}) all-reduce(f32[512]{0:T(512)S(1)} %get-tuple-element.27, f32[512]{0:T(512)S(1)} %get-tuple-element.26), channel_id=1, replica_groups=mesh['crops'=8,'rows'=4] {'crops','rows'}, use_global_device_ids=true, to_apply=%region_56.57 | all-reduce | flops 1024 | bytes 8192 | tf_op jit(solution)/shard_map/psum | solution.py:42
  718.4 8.9 fusion.80
  756.5 10.2 fusion.83
  766.7 44.4 %all-reduce.5 = (f32[]{:T(128)}, f32[512]{0:T(512)S(1)}, f32[512]{0:T(512)S(1)}) all-reduce(f32[]{:T(128)S(6)} %div.220, f32[512]{0:T(512)S(1)} %get-tuple-element.25, f32[512]{0:T(512)S(1)} %get-tuple-element.24), channel_id=1, replica_groups=mesh['crops'=8,'rows'=4] {'crops','rows'}, use_global_device_ids=true, to_apply=%region_42.43 | all-reduce | flops 1025 | bytes 8200 | tf_op jit(solution)/shard_map/psum | solution.py:194
  823.4 13.3 fusion.98
  837.7 16.8 %fusion.58 = f32[2048,2048]{1,0:T(8,128)} fusion(f32[36,2048]{1,0:T(8,128)S(1)} %copy-done.9, u32[]{:S(6)} %subtract, f32[20]{0:T(128)S(1)} %copy-done.43, f32[20,2048]{1,0:T(8,128)S(1)} %get-tuple-element.112, f32[20,2048]{1,0:T(8,128)S(1)} %get-tuple-element.104, f32[]{:T(128)} %get-tuple-element.48, f32[2048]{0:T(1024)S(1)} %get-tuple-element.129, ...), kind=kOutput, calls=%fused_computation.144 | convolution fusion | flops 1006960640 | bytes 17408520 | tf_op jit(solution)/shard_map/dot_general | solution.py:208
  859.2 52.8 %reduce-scatter.8.cloned.1.call-done = f32[256,512]{1,0:T(8,128)} async-done(((f32[2048,512]{1,0:T(8,128)}), f32[256,512]{1,0:T(8,128)}) %reduce-scatter.8.cloned.1.call-update) | async-done | bytes 524304 | tf_op jit(solution)/shard_map/reduce_scatter | solution.py:269
  912.0 167.3 %reduce-scatter.10.cloned.1.call-done = f32[576,512]{1,0:T(8,128)} async-done(((f32[4608,512]{1,0:T(8,128)}), f32[576,512]{1,0:T(8,128)}) %reduce-scatter.10.cloned.1.call-update) | async-done | bytes 1179664 | tf_op jit(solution)/shard_map/reduce_scatter | solution.py:270
  1079.2 285.3 %reduce-scatter.14.cloned.1.call-done = f32[256,2048]{1,0:T(8,128)} async-done(((f32[2048,2048]{1,0:T(8,128)}), f32[256,2048]{1,0:T(8,128)}) %reduce-scatter.14.cloned.1.call-update) | async-done | bytes 2097168 | tf_op jit(solution)/shard_map/reduce_scatter | solution.py:272
  1372.3 128.8 %all-reduce.17.cloned.1.call-done = f32[128,3000]{0,1:T(8,128)} async-done(((f32[128,3000]{0,1:T(8,128)}), f32[128,3000]{0,1:T(8,128)}) %all-reduce.17.cloned.1.call-update) | async-done | bytes 1536016 | tf_op jit(solution)/shard_map/psum | solution.py:194
  1501.1 92.4 %all-reduce.19.cloned.1.call-done = (f32[256,512]{1,0:T(8,128)}, f32[576,512]{1,0:T(8,128)}, f32[64,2048]{1,0:T(8,128)}, f32[256,2048]{1,0:T(8,128)}, f32[256,128]{1,0:T(8,128)}) async-done(((f32[256,512]{1,0:T(8,128)}, f32[576,512]{1,0:T(8,128)}, f32[64,2048]{1,0:T(8,128)}, f32[256,2048]{1,0:T(8,128)}, f32[256,128]{1,0:T(8,128)}), (f32[256,512]{1,0:T(8,128)}, f32[576,512]{1,0:T(8,128)}, ...) | async-done | bytes 4456464 | tf_op jit(solution)/shard_map/psum | solution.py:275
  (308 shorter events, 165.9 us)
Async XLA Ops:
  7.2 160.4 %copy-start = (f32[128,3000]{0,1:T(8,128)S(1)}, f32[128,3000]{0,1:T(8,128)}, u32[]{:S(2)}) copy-start(f32[128,3000]{0,1:T(8,128)} %param.27) | copy-start | bytes 4608004
  7.2 55.0 %all-gather.7.cloned.1.call-start = ((), (), s32[]{:S(2)}) async-start(), calls=%async_computation.5 | async-start | bytes 2359296 | tf_op jit(solution)/shard_map/all_gather | solution.py:127
  7.9 181.2 %all-gather.9.cloned.1.call-start = ((), (), s32[]{:S(2)}) async-start(), calls=%async_computation.6 | async-start | bytes 5308416 | tf_op jit(solution)/shard_map/all_gather | solution.py:128
  8.7 236.3 %all-gather.11.cloned.1.call-start = ((), (), s32[]{:S(2)}) async-start(), calls=%async_computation.7 | async-start | bytes 2359296 | tf_op jit(solution)/shard_map/all_gather | solution.py:129
  9.4 330.8 %all-gather.13.cloned.1.call-start = ((), (), s32[]{:S(2)}) async-start(), calls=%async_computation.8 | async-start | bytes 9437184 | tf_op jit(solution)/shard_map/all_gather | solution.py:130
  10.0 849.1 %reduce-scatter.16.cloned.1.call-start = ((), (), s32[]{:S(2)}) async-start(), calls=%async_computation.13 | async-start | bytes 1179648 | tf_op jit(solution)/shard_map/reduce_scatter | solution.py:273
  111.8 70.2 %copy-start.29 = (f32[512]{0:T(512)}, f32[512]{0:T(512)S(1)}, u32[]{:S(2)}) copy-start(f32[512]{0:T(512)S(1)} %get-tuple-element.63) | copy-start | bytes 6148
  111.8 70.2 %copy-start.31 = (f32[512]{0:T(512)}, f32[512]{0:T(512)S(1)}, u32[]{:S(2)}) copy-start(f32[512]{0:T(512)S(1)} %get-tuple-element.98) | copy-start | bytes 6148
  114.8 52.8 %copy-start.15 = (f32[120,128]{1,0:T(8,128)S(1)}, f32[120,128]{1,0:T(8,128)}, u32[]{:S(2)}) copy-start(f32[120,128]{1,0:T(8,128)} %param.21) | copy-start | bytes 184324
  117.0 52.8 %collective-permute-start = (bf16[80,1,8,512]{3,2,1,0:T(8,128)(2,1)}, bf16[80,1,8,512]{3,2,1,0:T(8,128)(2,1)}, u32[]{:S(2)}, u32[]{:S(2)}) collective-permute-start(bf16[80,1,8,512]{3,2,1,0:T(8,128)(2,1)} %get-tuple-element.89), channel_id=1, source_target_pairs={{0,1},{1,2},{2,3},{4,5},{5,6},{6,7},{8,9},{9,10},{10,11},{12,13},{... | collective-permute-start | bytes 1966088 | tf_op jit(solution)/shard_map/ppermute | solution.py:21
  119.8 50.1 %collective-permute-start.1 = (bf16[80,1,8,512]{3,2,1,0:T(8,128)(2,1)}, bf16[80,1,8,512]{3,2,1,0:T(8,128)(2,1)}, u32[]{:S(2)}, u32[]{:S(2)}) collective-permute-start(bf16[80,1,8,512]{3,2,1,0:T(8,128)(2,1)} %get-tuple-element.90), channel_id=1, source_target_pairs={{1,0},{2,1},{3,2},{5,4},{6,5},{7,6},{9,8},{10,9},{11,10},{13,12},{... | collective-permute-start | bytes 1966088 | tf_op jit(solution)/shard_map/ppermute | solution.py:23
  132.5 207.8 %copy-start.41 = (f32[20]{0:T(128)}, f32[20]{0:T(128)S(1)}, u32[]{:S(2)}) copy-start(f32[20]{0:T(128)S(1)} %dynamic-slice.3) | copy-start | bytes 244
  189.2 54.5 %copy-start.75 = (f32[512]{0:T(512)S(1)}, f32[512]{0:T(512)}, u32[]{:S(2)}) copy-start(f32[512]{0:T(512)} %param.30) | copy-start | bytes 6148
  189.2 55.8 %copy-start.80 = (f32[512]{0:T(512)S(1)}, f32[512]{0:T(512)}, u32[]{:S(2)}) copy-start(f32[512]{0:T(512)} %param.31) | copy-start | bytes 6148
  244.9 54.6 %copy-start.23 = (f32[2048]{0:T(1024)S(1)}, f32[2048]{0:T(1024)}, u32[]{:S(2)}) copy-start(f32[2048]{0:T(1024)} %param.32) | copy-start | bytes 24580
  244.9 56.5 %copy-start.33 = (f32[2048]{0:T(1024)S(1)}, f32[2048]{0:T(1024)}, u32[]{:S(2)}) copy-start(f32[2048]{0:T(1024)} %param.33) | copy-start | bytes 24580
  335.7 2.3 collective-permute-start.4
  340.2 51.5 %copy-start.35 = (f32[2048]{0:T(1024)S(1)}, f32[2048]{0:T(1024)}, u32[]{:S(2)}) copy-start(f32[2048]{0:T(1024)} %param.34) | copy-start | bytes 24580
  340.2 52.8 %copy-start.57 = (f32[2048]{0:T(1024)S(1)}, f32[2048]{0:T(1024)}, u32[]{:S(2)}) copy-start(f32[2048]{0:T(1024)} %param.35) | copy-start | bytes 24580
  587.7 249.1 %copy-start.37 = (f32[2048]{0:T(1024)}, f32[2048]{0:T(1024)S(1)}, u32[]{:S(2)}) copy-start(f32[2048]{0:T(1024)S(1)} %get-tuple-element.129) | copy-start | bytes 24580
  587.7 249.1 %copy-start.38 = (f32[2048]{0:T(1024)}, f32[2048]{0:T(1024)S(1)}, u32[]{:S(2)}) copy-start(f32[2048]{0:T(1024)S(1)} %get-tuple-element.130) | copy-start | bytes 24580
  606.9 55.5 %copy-start.28 = (f32[2048]{0:T(1024)S(1)}, f32[2048]{0:T(1024)}, u32[]{:S(2)}) copy-start(f32[2048]{0:T(1024)} %get-tuple-element.66) | copy-start | bytes 24580
  606.9 252.3 %reduce-scatter.12.cloned.1.call-start = ((), (), s32[]{:S(2)}) async-start(), calls=%async_computation.11 | async-start | bytes 4718592 | tf_op jit(solution)/shard_map/reduce_scatter | solution.py:271
  727.3 184.7 %reduce-scatter.8.cloned.1.call-start = ((), (), s32[]{:S(2)}) async-start(), calls=%async_computation.9 | async-start | bytes 4718592 | tf_op jit(solution)/shard_map/reduce_scatter | solution.py:269
  733.3 12.7 collective-permute-start.2
  734.8 11.2 collective-permute-start.3
  756.5 54.6 %copy-start.51 = (f32[512]{0:T(512)S(1)}, f32[512]{0:T(512)}, u32[]{:S(2)}) copy-start(f32[512]{0:T(512)} %get-tuple-element.62) | copy-start | bytes 6148
  823.3 255.9 %reduce-scatter.10.cloned.1.call-start = ((), (), s32[]{:S(2)}) async-start(), calls=%async_computation.10 | async-start | bytes 10616832 | tf_op jit(solution)/shard_map/reduce_scatter | solution.py:270
  836.7 527.8 %reduce-scatter.14.cloned.1.call-start = ((), (), s32[]{:S(2)}) async-start(), calls=%async_computation.12 | async-start | bytes 18874368 | tf_op jit(solution)/shard_map/reduce_scatter | solution.py:272
  854.6 646.6 %all-reduce.17.cloned.1.call-start = ((), (), s32[]{:S(2)}) async-start(), calls=%async_computation.14 | async-start | bytes 3072000 | tf_op jit(solution)/shard_map/psum | solution.py:194
  859.0 505.5 %copy-start.12 = (bf16[1280,512]{1,0:T(8,128)(2,1)S(1)}, bf16[1280,512]{1,0:T(8,128)(2,1)}, u32[]{:S(2)}) copy-start(bf16[1280,512]{1,0:T(8,128)(2,1)} %copy-done.11) | copy-start | bytes 3932164
  859.1 734.4 %all-reduce.19.cloned.1.call-start = ((), (), s32[]{:S(2)}) async-start(), calls=%async_computation.15 | async-start | bytes 8912896 | tf_op jit(solution)/shard_map/psum | solution.py:275
  (70 other events, 640.1 us)
Sparse Core Ops, SparseCore 0:
  10.2 51.9 all-gather.6
  64.4 80.9 all-gather.8
  147.5 48.5 all-gather.10
  198.1 125.5 all-gather.12
  607.0 63.1 reduce-scatter.15
  727.4 88.6 reduce-scatter.11
  823.4 88.4 reduce-scatter.7
  916.0 163.1 reduce-scatter.9
  1083.5 280.9 reduce-scatter.13
  1370.2 130.8 all-reduce.16
  1503.8 89.6 all-reduce.18
where the time goes:
time: 1620 us; the launch traced here: 1610 us
  waiting for transfers between devices  773 us (48%)
  blocking collectives  538 us (33%)
  matrix products  128 us (8%)
  other arithmetic  95 us (6%)
  local copies, waits for them, and re-layouts  48.3 us (3%)
  between operations  17.2 us (1%)
    reduce_scatter x1, waiting for transfers between devices, shards(): lax.psum_scatter(grad_w_hidden, 'crops', scatter_dimension=0, tiled=True)  285 us
    psum x4, blocking collectives, moments(): lax.psum((first_sum, second_sum, jnp.sum(weights)), ('crops', 'rows'))  175 us
    reduce_scatter x1, waiting for transfers between devices, shards(): lax.psum_scatter(grad_w_spatial, 'crops', scatter_dimension=0, tiled=True)  167 us
    psum x1, waiting for transfers between devices, shards(): lax.psum((jnp.sum(grad_act_head * norm_head, axis=0), jnp.sum(grad_act_he...  129 us
    psum x3, blocking collectives, shards(): lax.psum(jnp.sum(plan_mass, axis=0) + jnp.sum(queue_mass, axis=0), ('crop...  122 us
    psum x1, waiting for transfers between devices, shards(): lax.psum((sum_reduce, sum_spatial, sum_expand, sum_hidden, sum_embed), 'r...  92.4 us
    psum x2, blocking collectives, shards(): lax.psum((jnp.sum(grad_act_head * norm_head, axis=0), jnp.sum(grad_act_he...  82.4 us
    psum x2, blocking collectives, norm_back(): lax.psum((jnp.sum(upstream * normed, axis=0), jnp.sum(upstream, axis=0)),...  79.6 us
  transfers between devices with their start and end apart: 16, of which 7 were waited for; matrix products, arithmetic and copies ran while one was open for 14% of the time, Pallas kernels for 0%

commit v1 on v0

--- a/solution.py
+++ b/solution.py
@@ -162,9 +162,8 @@
     plan_mass = jnp.exp(centroid_similarity / SHARPNESS)
     queue_mass = jnp.exp(stored_similarity / SHARPNESS)
     for iteration in range(3):
-        column = lax.psum(
-            jnp.sum(plan_mass, axis=0) + jnp.sum(queue_mass, axis=0), ("crops", "rows")
-        )
+        u_in = jnp.sum(plan_mass, axis=0) + jnp.sum(queue_mass, axis=0)
+        column = lax.all_gather(u_in, axis_name=("crops", "rows")).sum(axis=0)
         plan_mass = plan_mass / (proto_total * column)
         queue_mass = queue_mass / (proto_total * column)
         plan_mass = plan_mass / (row_total * jnp.sum(plan_mass, axis=1, keepdims=True))

time: 1620 us -> 1870 us (1.15)
  waiting for transfers between devices: 773 us -> 1160 us
  blocking collectives: 538 us -> 402 us
    unnamed x12 -> x18, waiting for transfers between devices: 3.06 us -> 383 us
    psum x3 -> x0, blocking collectives: 122 us -> none  [shards(): lax.psum(jnp.sum(plan_mass, axis=0) + jnp.sum(queue_mass, axis=0), ('crop...]
  transfers between devices with their start and end apart: 16 -> 19, of which waited for: 7 -> 11; matrix products, arithmetic and copies ran while one was open for 14% -> 12% of each run, Pallas kernels for 0% -> 0%
where the time goes in v1:
time: 1870 us
  waiting for transfers between devices  1160 us (62%)
  blocking collectives  402 us (21%)
  matrix products  128 us (7%)
  other arithmetic  96.4 us (5%)
  local copies, waits for them, and re-layouts  53 us (3%)
    unnamed x18, waiting for transfers between devices  383 us
    reduce_scatter x1, waiting for transfers between devices, shards(): lax.psum_scatter(grad_w_hidden, 'crops', scatter_dimension=0, tiled=True)  285 us
    reduce_scatter x1, waiting for transfers between devices, shards(): lax.psum_scatter(grad_w_spatial, 'crops', scatter_dimension=0, tiled=True)  167 us
    psum x4, blocking collectives, moments(): lax.psum((first_sum, second_sum, jnp.sum(weights)), ('crops', 'rows'))  164 us
    psum x1, waiting for transfers between devices, shards(): lax.psum((jnp.sum(grad_act_head * norm_head, axis=0), jnp.sum(grad_act_he...  130 us
    psum x1, waiting for transfers between devices, shards(): lax.psum((sum_reduce, sum_spatial, sum_expand, sum_hidden, sum_embed), 'r...  92.4 us
    psum x2, blocking collectives, shards(): lax.psum((jnp.sum(grad_act_head * norm_head, axis=0), jnp.sum(grad_act_he...  83.2 us
    psum x2, blocking collectives, norm_back(): lax.psum((jnp.sum(upstream * normed, axis=0), jnp.sum(upstream, axis=0)),...  78.5 us
  transfers between devices with their start and end apart: 19, of which 11 were waited for; matrix products, arithmetic and copies ran while one was open for 12% of the time, Pallas kernels for 0%

profile of v1, /device:TPU:0, one launch (start us, length us, event | category | flops | bytes accessed | tf_op | source)
XLA Modules:
  0.0 1865.1 jit_solution(13753655326703362011)
XLA Ops:
  17.8 44.4 %all-gather.10.cloned.1.call-done = bf16[2048,512]{1,0:T(8,128)(2,1)} async-done(((bf16[256,512]{1,0:T(8,128)(2,1)}), bf16[2048,512]{1,0:T(8,128)(2,1)}) %all-gather.10.cloned.1.call-update) | async-done | bytes 2097168 | tf_op jit(solution)/shard_map/all_gather | solution.py:127
  69.9 40.6 %all-reduce.15 = (f32[512]{0:T(512)S(1)}, f32[]{:T(128)}, f32[512]{0:T(512)S(1)}) all-reduce(f32[512]{0:T(512)S(1)} %get-tuple-element.23, f32[]{:T(128)} %convert_reduce_fusion, f32[512]{0:T(512)S(1)} %get-tuple-element.22), channel_id=1, replica_groups=mesh['crops'=8,'rows'=4] {'crops','rows'}, use_global_device_ids=true, to_apply=%region_5.0 | all-reduce | flops 1025 | bytes 8200 | tf_op jit(solution)/shard_map/psum | solution.py:33
  144.1 11.6 multiply_reduce_fusion.6
  155.7 43.0 %all-reduce.14 = (f32[512]{0:T(512)S(1)}, f32[512]{0:T(512)S(1)}) all-reduce(f32[512]{0:T(512)S(1)} %get-tuple-element.21, f32[512]{0:T(512)S(1)} %get-tuple-element.20), channel_id=1, replica_groups=mesh['crops'=8,'rows'=4] {'crops','rows'}, use_global_device_ids=true, to_apply=%region_9.10 | all-reduce | flops 1024 | bytes 8192 | tf_op jit(solution)/shard_map/psum | solution.py:33
  200.0 9.1 multiply_reduce_fusion.1
  209.1 42.0 %all-reduce.13 = (f32[2048]{0:T(1024)S(1)}, f32[2048]{0:T(1024)S(1)}) all-reduce(f32[2048]{0:T(1024)S(1)} %get-tuple-element.17, f32[2048]{0:T(1024)S(1)} %get-tuple-element.16), channel_id=1, replica_groups=mesh['crops'=8,'rows'=4] {'crops','rows'}, use_global_device_ids=true, to_apply=%region_11.12 | all-reduce | flops 4096 | bytes 32768 | tf_op jit(solution)/shard_map/psum | solution.py:33
  253.2 13.4 multiply_multiply_fusion.2
  273.7 13.9 fusion
  289.0 35.4 %all_gather.37 = bf16[2048,128]{1,0:T(8,128)(2,1)} all-gather(bf16[256,128]{1,0:T(8,128)(2,1)} %param.26), channel_id=1, replica_groups=mesh['crops'=8,'rows'=4] {'crops'}, dimensions={0}, use_global_device_ids=true | all-gather | bytes 589824 | tf_op jit(solution)/shard_map/all_gather | solution.py:131
  340.3 38.7 %all-reduce.12 = (f32[2048]{0:T(1024)S(1)}, f32[]{:T(128)}, f32[2048]{0:T(1024)S(1)}) all-reduce(f32[2048]{0:T(1024)S(1)} %get-tuple-element.37, f32[]{:T(128)} %constant.39.clone.1, f32[2048]{0:T(1024)S(1)} %get-tuple-element.36), channel_id=1, replica_groups=mesh['crops'=8,'rows'=4] {'crops','rows'}, use_global_device_ids=true, to_apply=%region_22.23 | all-reduce | flops 4097 | bytes 32776 | tf_op jit(solution)/shard_map/psum | solution.py:33
  385.6 128.0 %all-reduce.25.cloned.1.call-done = f32[96000]{0:T(1024)} async-done(((f32[96000]{0:T(1024)}), f32[96000]{0:T(1024)}) %all-reduce.25.cloned.1.call-update) | async-done | bytes 384016
  522.4 126.5 %all-reduce.27.cloned.1.call-done = f32[96000]{0:T(1024)} async-done(((f32[96000]{0:T(1024)}), f32[96000]{0:T(1024)}) %all-reduce.27.cloned.1.call-update) | async-done | bytes 384016
  659.6 125.3 %all-reduce.29.cloned.1.call-done = f32[96000]{0:T(1024)} async-done(((f32[96000]{0:T(1024)}), f32[96000]{0:T(1024)}) %all-reduce.29.cloned.1.call-update) | async-done | bytes 384016
  788.0 11.1 all-gather.3
  806.7 39.5 %all-reduce.11 = (f32[2048]{0:T(1024)S(1)}, f32[2048]{0:T(1024)S(1)}) all-reduce(f32[2048]{0:T(1024)S(1)} %get-tuple-element.35, f32[2048]{0:T(1024)S(1)} %get-tuple-element.34), channel_id=1, replica_groups=mesh['crops'=8,'rows'=4] {'crops','rows'}, use_global_device_ids=true, to_apply=%region_48.49 | all-reduce | flops 4096 | bytes 32768 | tf_op jit(solution)/shard_map/psum | solution.py:193
  846.2 9.6 fusion.27
  855.8 9.4 all-gather.4
  865.8 15.0 fusion.82
  880.9 38.5 %all-reduce.10 = (f32[2048]{0:T(1024)S(1)}, f32[2048]{0:T(1024)S(1)}) all-reduce(f32[2048]{0:T(1024)S(1)} %get-tuple-element.19, f32[2048]{0:T(1024)S(1)} %get-tuple-element.18), channel_id=1, replica_groups=mesh['crops'=8,'rows'=4] {'crops','rows'}, use_global_device_ids=true, to_apply=%region_52.53 | all-reduce | flops 4096 | bytes 32768 | tf_op jit(solution)/shard_map/psum | solution.py:42
  919.5 10.0 multiply_convert_fusion.1
  935.9 40.0 %all-reduce.9 = (f32[512]{0:T(512)S(1)}, f32[512]{0:T(512)S(1)}) all-reduce(f32[512]{0:T(512)S(1)} %get-tuple-element.27, f32[512]{0:T(512)S(1)} %get-tuple-element.26), channel_id=1, replica_groups=mesh['crops'=8,'rows'=4] {'crops','rows'}, use_global_device_ids=true, to_apply=%region_56.57 | all-reduce | flops 1024 | bytes 8192 | tf_op jit(solution)/shard_map/psum | solution.py:42
  975.9 8.9 fusion.80
  1014.1 10.2 fusion.83
  1024.3 43.7 %all-reduce.8 = (f32[]{:T(128)}, f32[512]{0:T(512)S(1)}, f32[512]{0:T(512)S(1)}) all-reduce(f32[]{:T(128)S(6)} %div.220, f32[512]{0:T(512)S(1)} %get-tuple-element.25, f32[512]{0:T(512)S(1)} %get-tuple-element.24), channel_id=1, replica_groups=mesh['crops'=8,'rows'=4] {'crops','rows'}, use_global_device_ids=true, to_apply=%region_42.43 | all-reduce | flops 1025 | bytes 8200 | tf_op jit(solution)/shard_map/psum | solution.py:193
  1080.4 13.3 fusion.98
  1094.7 16.8 fusion.58
  1116.1 52.4 %reduce-scatter.8.cloned.1.call-done = f32[256,512]{1,0:T(8,128)} async-done(((f32[2048,512]{1,0:T(8,128)}), f32[256,512]{1,0:T(8,128)}) %reduce-scatter.8.cloned.1.call-update) | async-done | bytes 524304 | tf_op jit(solution)/shard_map/reduce_scatter | solution.py:268
  1168.5 166.8 %reduce-scatter.10.cloned.1.call-done = f32[576,512]{1,0:T(8,128)} async-done(((f32[4608,512]{1,0:T(8,128)}), f32[576,512]{1,0:T(8,128)}) %reduce-scatter.10.cloned.1.call-update) | async-done | bytes 1179664 | tf_op jit(solution)/shard_map/reduce_scatter | solution.py:269
  1335.3 284.6 %reduce-scatter.14.cloned.1.call-done = f32[256,2048]{1,0:T(8,128)} async-done(((f32[2048,2048]{1,0:T(8,128)}), f32[256,2048]{1,0:T(8,128)}) %reduce-scatter.14.cloned.1.call-update) | async-done | bytes 2097168 | tf_op jit(solution)/shard_map/reduce_scatter | solution.py:271
  1619.9 7.8 multiply_convert_fusion
  1627.8 129.8 %all-reduce.23.cloned.1.call-done = f32[128,3000]{0,1:T(8,128)} async-done(((f32[128,3000]{0,1:T(8,128)}), f32[128,3000]{0,1:T(8,128)}) %all-reduce.23.cloned.1.call-update) | async-done | bytes 1536016 | tf_op jit(solution)/shard_map/psum | solution.py:193
  1757.6 92.4 %all-reduce.31.cloned.1.call-done = (f32[256,512]{1,0:T(8,128)}, f32[576,512]{1,0:T(8,128)}, f32[64,2048]{1,0:T(8,128)}, f32[256,2048]{1,0:T(8,128)}, f32[256,128]{1,0:T(8,128)}) async-done(((f32[256,512]{1,0:T(8,128)}, f32[576,512]{1,0:T(8,128)}, f32[64,2048]{1,0:T(8,128)}, f32[256,2048]{1,0:T(8,128)}, f32[256,128]{1,0:T(8,128)}), (f32[256,512]{1,0:T(8,128)}, f32[576,512]{1,0:T(8,128)}, ...) | async-done | bytes 4456464 | tf_op jit(solution)/shard_map/psum | solution.py:274
  (315 shorter events, 175.8 us)
Async XLA Ops:
  7.2 111.8 %copy-start = (f32[128,3000]{0,1:T(8,128)S(1)}, f32[128,3000]{0,1:T(8,128)}, u32[]{:S(2)}) copy-start(f32[128,3000]{0,1:T(8,128)} %param.27) | copy-start | bytes 4608004
  7.2 55.0 %all-gather.10.cloned.1.call-start = ((), (), s32[]{:S(2)}) async-start(), calls=%async_computation.5 | async-start | bytes 2359296 | tf_op jit(solution)/shard_map/all_gather | solution.py:127
  7.9 136.2 %all-gather.12.cloned.1.call-start = ((), (), s32[]{:S(2)}) async-start(), calls=%async_computation.6 | async-start | bytes 5308416 | tf_op jit(solution)/shard_map/all_gather | solution.py:128
  8.7 191.3 %all-gather.14.cloned.1.call-start = ((), (), s32[]{:S(2)}) async-start(), calls=%async_computation.7 | async-start | bytes 2359296 | tf_op jit(solution)/shard_map/all_gather | solution.py:129
  9.4 324.9 %all-gather.16.cloned.1.call-start = ((), (), s32[]{:S(2)}) async-start(), calls=%async_computation.8 | async-start | bytes 9437184 | tf_op jit(solution)/shard_map/all_gather | solution.py:130
  10.0 503.6 %all-reduce.25.cloned.1.call-start = ((), (), s32[]{:S(2)}) async-start(), calls=%async_computation.15 | async-start | bytes 770048
  115.0 6.3 collective-permute-start
  117.0 6.0 collective-permute-start.1
  139.7 59.0 %copy-start.72 = (f32[512]{0:T(512)S(1)}, f32[512]{0:T(512)}, u32[]{:S(2)}) copy-start(f32[512]{0:T(512)} %param.30) | copy-start | bytes 6148
  139.7 60.3 %copy-start.76 = (f32[512]{0:T(512)S(1)}, f32[512]{0:T(512)}, u32[]{:S(2)}) copy-start(f32[512]{0:T(512)} %param.31) | copy-start | bytes 6148
  266.6 57.9 %copy-start.74 = (u32[32]{0:T(128)S(1)}, u32[32]{0:T(128)}, u32[]{:S(2)}) copy-start(u32[32]{0:T(128)} %constant.114) | copy-start | bytes 388
  287.7 44.4 %collective-permute-start.4 = (f32[12,2048]{1,0:T(8,128)S(1)}, f32[12,2048]{1,0:T(8,128)S(1)}, u32[]{:S(2)}, u32[]{:S(2)}) collective-permute-start(f32[12,2048]{1,0:T(8,128)S(1)} %slice.121), channel_id=1, source_target_pairs={{0,1},{1,2},{2,3},{4,5},{5,6},{6,7},{8,9},{9,10},{10,11},{12,13},{... | collective-permute-start | bytes 294920
  380.2 135.4 %copy-start.18 = (f32[2048]{0:T(1024)}, f32[2048]{0:T(1024)S(1)}, u32[]{:S(2)}) copy-start(f32[2048]{0:T(1024)S(1)} %get-tuple-element.92) | copy-start | bytes 24580
  380.2 135.4 %copy-start.20 = (f32[2048]{0:T(1024)}, f32[2048]{0:T(1024)S(1)}, u32[]{:S(2)}) copy-start(f32[2048]{0:T(1024)S(1)} %get-tuple-element.93) | copy-start | bytes 24580
  381.8 136.4 %copy-start.58 = (f32[20]{0:T(128)}, f32[20]{0:T(128)S(1)}, u32[]{:S(2)}) copy-start(f32[20]{0:T(128)S(1)} %add_rsqrt_fusion.5) | copy-start | bytes 244
  383.4 135.6 %copy-start.43 = (f32[20]{0:T(128)}, f32[20]{0:T(128)S(1)}, u32[]{:S(2)}) copy-start(f32[20]{0:T(128)S(1)} %get-tuple-element.32) | copy-start | bytes 244
  385.6 263.4 %all-reduce.27.cloned.1.call-start = ((), (), s32[]{:S(2)}) async-start(), calls=%async_computation.16 | async-start | bytes 770048
  522.2 262.7 %all-reduce.29.cloned.1.call-start = ((), (), s32[]{:S(2)}) async-start(), calls=%async_computation.17 | async-start | bytes 770048
  658.1 458.0 %reduce-scatter.16.cloned.1.call-start = ((), (), s32[]{:S(2)}) async-start(), calls=%async_computation.13 | async-start | bytes 1179648 | tf_op jit(solution)/shard_map/reduce_scatter | solution.py:272
  658.9 143.1 %copy-start.61 = (pred[20]{0:T(512)(128)(4,1)}, pred[20]{0:T(512)(128)(4,1)S(1)}, u32[]{:S(2)}) copy-start(pred[20]{0:T(512)(128)(4,1)S(1)} %get-tuple-element.69) | copy-start | bytes 64
  659.6 142.5 %copy-start.64 = (f32[20]{0:T(128)}, f32[20]{0:T(128)S(1)}, u32[]{:S(2)}) copy-start(f32[20]{0:T(128)S(1)} %log.9) | copy-start | bytes 244
  846.2 247.6 %copy-start.35 = (f32[2048]{0:T(1024)}, f32[2048]{0:T(1024)S(1)}, u32[]{:S(2)}) copy-start(f32[2048]{0:T(1024)S(1)} %get-tuple-element.129) | copy-start | bytes 24580
  846.2 247.6 %copy-start.36 = (f32[2048]{0:T(1024)}, f32[2048]{0:T(1024)S(1)}, u32[]{:S(2)}) copy-start(f32[2048]{0:T(1024)S(1)} %get-tuple-element.130) | copy-start | bytes 24580
  865.3 250.8 %reduce-scatter.12.cloned.1.call-start = ((), (), s32[]{:S(2)}) async-start(), calls=%async_computation.11 | async-start | bytes 4718592 | tf_op jit(solution)/shard_map/reduce_scatter | solution.py:270
  984.8 183.7 %reduce-scatter.8.cloned.1.call-start = ((), (), s32[]{:S(2)}) async-start(), calls=%async_computation.9 | async-start | bytes 4718592 | tf_op jit(solution)/shard_map/reduce_scatter | solution.py:268
  990.9 12.7 collective-permute-start.2
  992.4 11.2 collective-permute-start.3
  1080.3 255.0 %reduce-scatter.10.cloned.1.call-start = ((), (), s32[]{:S(2)}) async-start(), calls=%async_computation.10 | async-start | bytes 10616832 | tf_op jit(solution)/shard_map/reduce_scatter | solution.py:269
  1093.7 526.2 %reduce-scatter.14.cloned.1.call-start = ((), (), s32[]{:S(2)}) async-start(), calls=%async_computation.12 | async-start | bytes 18874368 | tf_op jit(solution)/shard_map/reduce_scatter | solution.py:271
  1111.6 646.0 %all-reduce.23.cloned.1.call-start = ((), (), s32[]{:S(2)}) async-start(), calls=%async_computation.14 | async-start | bytes 3072000 | tf_op jit(solution)/shard_map/psum | solution.py:193
  1116.0 503.9 %copy-start.11 = (bf16[1280,512]{1,0:T(8,128)(2,1)S(1)}, bf16[1280,512]{1,0:T(8,128)(2,1)}, u32[]{:S(2)}) copy-start(bf16[1280,512]{1,0:T(8,128)(2,1)} %copy-done.10) | copy-start | bytes 3932164
  1116.0 733.9 %all-reduce.31.cloned.1.call-start = ((), (), s32[]{:S(2)}) async-start(), calls=%async_computation.18 | async-start | bytes 8912896 | tf_op jit(solution)/shard_map/psum | solution.py:274
  (69 other events, 806.4 us)
Sparse Core Ops, SparseCore 0:
  10.2 51.9 all-gather.9
  64.4 79.6 all-gather.11
  146.2 47.5 all-gather.13
  195.8 129.6 all-gather.15
  385.7 127.8 all-reduce.24
  522.3 126.6 all-reduce.26
  658.2 126.6 all-reduce.28
  865.5 61.6 reduce-scatter.15
  984.9 88.2 reduce-scatter.11
  1080.4 87.9 reduce-scatter.7
  1172.1 163.1 reduce-scatter.9
  1338.9 280.9 reduce-scatter.13
  1626.6 130.8 all-reduce.22
  1760.3 89.6 all-reduce.30
